TPU v7x, 32 devices: a whole 2x2x4 slice. The times are simulated.
32 devices in a mesh: groups: 2 (over y), gx: 16 (over z, x, core).
Axes of the slice: x: 2, y: 2, z: 4, core: 2. Of those that a mesh axis runs over, the one named last changes fastest.
Arguments:
- activations: bfloat16 [128, 16, 16, 512], P(('groups', 'gx')), parts along dimension 0, may hold values from -6 to 6
- first_kernel: bfloat16 [3, 3, 3, 16, 32], replicated, may hold values from -0.3125 to 0.3125
- second_kernel: bfloat16 [3, 3, 3, 32, 64], replicated, may hold values from -0.21875 to 0.21875
- head_weight: float32 [64], replicated, may hold values from -1.5 to 1.5
- labels: int32 [32, 4, 128], P(('groups', 'gx')), parts along dimension 0, may hold values 0 or 1
Outputs:
- input_grad: bfloat16 [128, 16, 16, 512], P(('groups', 'gx')), parts along dimension 0
- first_grad: float32 [6, 3, 3, 16, 32], P('groups'), parts along dimension 0
- second_grad: float32 [6, 3, 3, 32, 64], P('groups'), parts along dimension 0
- head_grad: float32 [128], P('groups'), parts along dimension 0
There are 2 independent parts, one for each index of `groups`. A program takes and returns all parts, laid end to end along the dimension named above; an argument that names none is the same for every part. Nothing has to cross between parts.
All inputs are finite; a program needn't handle non-finite values. No bound on the sum of `labels` on one device may be relied on, other than what follows from the above.
Results may differ from a plain program's by a relative error of at most 0.0062.
Values may be sent and summed in bfloat16 or wider, within the bound.
A program may use at most 128 MiB of HBM per device.

v0:
```python
import functools

import jax
import jax.numpy as jnp
from jax import lax
from jax.experimental import pallas as pl
from jax.experimental.pallas import tpu as pltpu
from jax.sharding import PartitionSpec as P

F32 = jnp.float32
BF16 = jnp.bfloat16
MESH = pl.DeviceIdType.MESH


def mm(left, right):
    return lax.dot_general(left, right, (((1,), (0,)), ((), ())), preferred_element_type=F32)


def mm_nt(left, right):
    return lax.dot_general(left, right, (((1,), (1,)), ((), ())), preferred_element_type=F32)


def iota(shape, axis):
    return lax.broadcasted_iota(jnp.int32, shape, axis)


def one_hot(condition):
    return jnp.where(condition, 1.0, 0.0).astype(BF16)


def each(count, body):
    def step(index, carry):
        body(index)
        return carry

    lax.fori_loop(0, count, step, 0, unroll=True)


def rows(start, size, align=16):
    return pl.ds(pl.multiple_of(start, align), size)


def roll_masked(value, shift, empty_lane):
    rolled = pltpu.roll(value, shift, axis=1)
    return jnp.where(iota(value.shape, 1) == empty_lane, 0.0, rolled)


def kernel(
    n, p1, p2, inverse_count,
    act, w1, w2, hw, labels,
    out, fg_out, sg_out, head_out,
    A, B, S2, SU, F2, slope1, IGp, spread, gather, w1t, w2t, bd1, bd2,
    abuf, sbuf, fbuf, halo_a, halo_b, halo_s, halo_f,
    G1, R1, T1, G2, R2, T2,
    halo_send, halo_recv, rs1_s, rs1_r, ag1_s, ag1_r, rs2_s, rs2_r, ag2_s, ag2_r,
):
    me = lax.axis_index("gx")
    group = lax.axis_index("groups")
    has_lower = me > 0
    has_upper = me < n - 1

    def partner(d):
        return lax.rem(me + d, n)

    barrier = pltpu.get_barrier_semaphore()

    def greet(d, carry):
        pl.semaphore_signal(barrier, inc=1, device_id=(group, partner(d)), device_id_type=MESH)
        return carry

    lax.fori_loop(1, n, greet, 0)

    z_row = iota((512, 640), 0)
    lane = iota((512, 640), 1)
    spread[...] = one_hot(z_row == 4 * (lane & 127) + (lane >> 7) - 1)
    src = iota((512, 512), 0)
    gather[...] = one_hot(iota((512, 512), 1) == 4 * (src & 127) + 2 * ((src >> 7) & 1) + (src >> 8))

    pl.semaphore_wait(barrier, n - 1)

    def halo(slot, source, target, to):
        return pltpu.make_async_remote_copy(
            src_ref=source, dst_ref=target, send_sem=halo_send.at[slot], recv_sem=halo_recv.at[slot],
            device_id=(group, to), device_id_type=MESH,
        )

    up = lax.rem(me + 1, n)
    down = lax.rem(me + n - 1, n)
    send_a = halo(0, act.at[3], halo_a, up)
    send_b = halo(1, abuf, halo_b, up)
    send_s = halo(2, sbuf, halo_s, down)
    send_f = halo(3, fbuf, halo_f, down)

    @pl.when(has_upper)
    def _():
        send_a.start()

    eye32 = one_hot(iota((32, 32), 0) == iota((32, 32), 1))
    eye64 = one_hot(iota((64, 64), 0) == iota((64, 64), 1))
    for a in range(3):
        w1t[a] = mm_nt(eye32, w1[a * 144:(a + 1) * 144, :]).astype(BF16)
        w2t[a] = mm_nt(eye64, w2[a * 288:(a + 1) * 288, :]).astype(BF16)
    for place, a in enumerate((1, 2, 0)):
        def k1(b, c):
            at = (a * 9 + b * 3 + c) * 16
            return w1[at:at + 16, :].astype(F32)

        def k2(b, c):
            at = (a * 9 + b * 3 + c) * 32
            return w2[at:at + 32, :].astype(F32)

        zero1 = jnp.zeros((16, 32), F32)
        zero2 = jnp.zeros((32, 64), F32)
        for k, zero, dest, height in ((k1, zero1, bd1, 16), (k2, zero2, bd2, 32)):
            table = (
                (k(1, 1), zero, zero, zero),
                (k(1, 2), k(1, 0), zero, zero),
                (k(2, 1), zero, k(0, 1), zero),
                (k(2, 2), k(2, 0), k(0, 2), k(0, 0)),
            )
            for q, parts in enumerate(table):
                at = place * 4 * height + q * height
                dest[at:at + height, :] = jnp.concatenate(parts, axis=1).astype(BF16)

    for x in range(5):
        A[x, 0:48, :] = jnp.zeros((48, 256), BF16)
    for x in range(3):
        B[x, 0:96, :] = jnp.zeros((96, 128), BF16)
        F2[x, 512:576, :] = jnp.zeros((64, 256), BF16)
    S2[512:640, :] = jnp.zeros((128, 128), BF16)
    SU[512:640, :] = jnp.zeros((128, 128), BF16)

    def fill_a(x, plane):
        phases = mm(plane, spread[...]).astype(BF16)
        for y in range(16):
            part = phases[y * 16:(y + 1) * 16, :]
            for c in range(3):
                at = (y + 1) * 48 + c * 16
                A[x, at:at + 16, 0:128] = part[:, c * 128:(c + 1) * 128]
                A[x, at:at + 16, 128:256] = part[:, (c + 2) * 128:(c + 3) * 128]

    def fill_b(x, j, value):
        even = value[:, 0:128]
        odd = value[:, 128:256]
        back = roll_masked(odd.astype(F32), 1, 0).astype(BF16)
        at = (j + 1) * 96
        B[x, rows(at, 32), :] = back
        B[x, rows(at + 32, 32), :] = even
        B[x, rows(at + 64, 32), :] = odd

    def first_section(i):
        def body(j):
            at = rows(j * 96, 144)
            pre = mm(w1t[0], A[2 * i, at, :]) + mm(w1t[1], A[2 * i + 1, at, :]) + mm(w1t[2], A[2 * i + 2, at, :])
            sig = jax.nn.sigmoid(pre)
            slope1[i, rows(j * 32, 32), :] = sig * (1.0 + pre * (1.0 - sig))
            value = (pre * sig).astype(BF16)
            if i == 1:
                abuf[rows(j * 32, 32), :] = value
            fill_b(i + 1, j, value)

        each(8, body)

    for x in (1, 2, 3):
        fill_a(x + 1, act[x])
    first_section(1)

    @pl.when(has_upper)
    def _():
        send_b.start()

    fill_a(1, act[0])

    @pl.when(has_lower)
    def _():
        send_a.wait_recv()
        fill_a(0, halo_a[...])

    @pl.when(jnp.logical_not(has_lower))
    def _():
        A[0] = jnp.zeros((816, 256), BF16)

    first_section(0)

    @pl.when(has_lower)
    def _():
        send_b.wait_recv()
        each(8, lambda j: fill_b(0, j, halo_b[rows(j * 32, 32), :]))

    @pl.when(jnp.logical_not(has_lower))
    def _():
        B[0] = jnp.zeros((864, 128), BF16)

    diagonal = iota((64, 64), 0) == iota((64, 64), 1)
    weight = jnp.sum(jnp.where(diagonal, hw[...], 0.0), axis=1, keepdims=True)

    def fill_s(target, j, value):
        at = j * 128
        target[rows(at, 64), :] = value
        target[rows(at + 64, 64), :] = roll_masked(value.astype(F32), 127, 127).astype(BF16)

    head = jnp.zeros((64, 128), F32)
    for j in range(4):
        at = slice(j * 192, j * 192 + 288)
        pre = mm(w2t[0], B[0, at, :]) + mm(w2t[1], B[1, at, :]) + mm(w2t[2], B[2, at, :])
        sig = jax.nn.sigmoid(pre)
        act2 = pre * sig
        logits = jnp.sum(act2 * weight, axis=0, keepdims=True)
        logit_grad = jax.nn.sigmoid(logits) - labels[0, j:j + 1, :].astype(F32)
        head = head + logit_grad * act2
        slope = (logit_grad * weight * (sig * (1.0 + pre * (1.0 - sig)))).astype(BF16)
        sbuf[j * 64:(j + 1) * 64, :] = slope
        fill_s(S2, j, slope)
    head = jnp.sum(head, axis=1, keepdims=True) * inverse_count

    @pl.when(has_lower)
    def _():
        send_s.start()

    def fill_f(plane, j, value):
        even = value[:, 0:128]
        ahead = roll_masked(even.astype(F32), 127, 127).astype(BF16)
        at = j * 64
        F2[plane, rows(at, 32), :] = value
        F2[plane, rows(at + 32, 32), 0:128] = value[:, 128:256]
        F2[plane, rows(at + 32, 32), 128:256] = ahead

    def first_back(plane, j, back):
        for q in range(2):
            at = (2 * j + q) * 32
            both = jnp.concatenate((back[q * 64:q * 64 + 32, :], back[q * 64 + 32:q * 64 + 64, :]), axis=1)
            value = (both * slope1[plane, rows(at, 32), :]).astype(BF16)
            if plane == 0:
                fbuf[rows(at, 32), :] = value
            fill_f(plane, 2 * j + q, value)

    each(4, lambda j: first_back(0, j, mm(bd2[0:128, :], S2[rows(j * 128, 256), :])))

    @pl.when(has_lower)
    def _():
        send_f.start()

    def scatter(G, R, s_sem, r_sem):
        def step(d, carry):
            to = partner(d)
            pltpu.make_async_remote_copy(
                src_ref=G.at[to], dst_ref=R.at[me], send_sem=s_sem.at[d], recv_sem=r_sem.at[me],
                device_id=(group, to), device_id_type=MESH,
            ).start()
            return carry

        lax.fori_loop(1, n, step, 0)
        R[me] = G[me]

    def gather_total(G, R, T, s_sem, r_sem, t_s, t_r):
        def arrive(d, carry):
            other = partner(d)
            pltpu.make_async_remote_copy(
                src_ref=G.at[other], dst_ref=R.at[other], send_sem=s_sem.at[d], recv_sem=r_sem.at[other],
                device_id=(group, other), device_id_type=MESH,
            ).wait()
            return carry

        lax.fori_loop(1, n, arrive, 0)
        T[me] = jnp.sum(R[...], axis=0)

        def step(d, carry):
            pltpu.make_async_remote_copy(
                src_ref=T.at[me], dst_ref=T.at[me], send_sem=t_s.at[d], recv_sem=t_r.at[me],
                device_id=(group, partner(d)), device_id_type=MESH,
            ).start()
            return carry

        lax.fori_loop(1, n, step, 0)

    def collect(T, t_s, t_r):
        def arrive(d, carry):
            other = partner(d)
            pltpu.make_async_remote_copy(
                src_ref=T.at[me], dst_ref=T.at[other], send_sem=t_s.at[d], recv_sem=t_r.at[other],
                device_id=(group, other), device_id_type=MESH,
            ).wait()
            return carry

        lax.fori_loop(1, n, arrive, 0)

    sums = []
    for a in range(3):
        total = jnp.zeros((288, 64), F32)
        for j in range(4):
            total = total + mm_nt(B[a, j * 192:j * 192 + 288, :], S2[j * 128:j * 128 + 64, :])
        sums.append(total * inverse_count)
    packed = jnp.concatenate(
        (
            jnp.concatenate((sums[0], sums[1][0:144, :]), axis=0),
            jnp.concatenate((sums[1][144:288, :], sums[2]), axis=0),
        ),
        axis=1,
    )
    packed = jnp.concatenate((packed, jnp.zeros((n * p2 - 432, 128), F32)), axis=0)
    G2[...] = packed.reshape(n, p2, 128)
    scatter(G2, R2, rs2_s, rs2_r)

    @pl.when(has_upper)
    def _():
        send_s.wait_recv()
        each(4, lambda j: fill_s(SU, j, halo_s[rows(j * 64, 64), :]))

    @pl.when(jnp.logical_not(has_upper))
    def _():
        SU[0:512, :] = jnp.zeros((512, 128), BF16)

    each(4, lambda j: first_back(
        1, j, mm(bd2[128:256, :], S2[rows(j * 128, 256), :]) + mm(bd2[256:384, :], SU[rows(j * 128, 256), :])))

    def first_grad(a):
        def step(j, total):
            for i in range(2):
                total = total + mm_nt(A[2 * i + a, rows(j * 96, 144), :], F2[i, rows(j * 64, 32), :])
            return total

        return lax.fori_loop(0, 8, step, jnp.zeros((144, 32), F32), unroll=True) * inverse_count

    head_column = jnp.concatenate((head, jnp.zeros((80, 1), F32)), axis=0)
    packed = jnp.concatenate(
        [first_grad(a) for a in range(3)] + [jnp.broadcast_to(head_column, (144, 32))], axis=1)
    packed = jnp.concatenate((packed, jnp.zeros((n * p1 - 144, 128), F32)), axis=0)
    G1[...] = packed.reshape(n, p1, 128)
    scatter(G1, R1, rs1_s, rs1_r)

    def put(x, j, value):
        value = value.astype(BF16)
        for q in range(2):
            for z in range(2):
                IGp[x, rows((2 * j + q) * 16, 16), z * 256:(z + 1) * 256] = value[q * 32 + z * 16:q * 32 + z * 16 + 16, :]

    def own_planes(j):
        at = rows(j * 64, 128)
        low = mm(bd1[0:128, :], F2[0, at, :])
        high = mm(bd1[...], F2[1, at, :])
        put(0, j, low[0:64, :])
        put(1, j, low[64:128, :] + high[128:192, :])
        put(2, j, high[0:64, :])

    each(8, own_planes)
    gather_total(G2, R2, T2, rs2_s, rs2_r, ag2_s, ag2_r)
    for x in range(3):
        out[x] = mm(IGp[x], gather[...]).astype(BF16)
    gather_total(G1, R1, T1, rs1_s, rs1_r, ag1_s, ag1_r)

    @pl.when(has_upper)
    def _():
        send_f.wait_recv()
        each(8, lambda j: fill_f(2, j, halo_f[rows(j * 32, 32), :]))

    @pl.when(jnp.logical_not(has_upper))
    def _():
        F2[2, 0:512, :] = jnp.zeros((512, 256), BF16)

    def last_plane(j):
        at = rows(j * 64, 128)
        put(3, j, mm(bd1[64:128, :], F2[1, at, :]) + mm(bd1[128:192, :], F2[2, at, :]))

    each(8, last_plane)
    out[3] = mm(IGp[3], gather[...]).astype(BF16)

    collect(T2, ag2_s, ag2_r)
    second = T2[...].reshape(n * p2, 128)
    sg_out[0:432, :] = second[0:432, 0:64]
    sg_out[432:864, :] = second[0:432, 64:128]
    collect(T1, ag1_s, ag1_r)
    first = T1[...].reshape(n * p1, 128)
    for a in range(3):
        fg_out[a * 144:(a + 1) * 144, :] = first[0:144, a * 32:(a + 1) * 32]
    head_out[...] = jnp.sum(jnp.where(diagonal, first[0:64, 96:97], 0.0), axis=0, keepdims=True)

    @pl.when(has_upper)
    def _():
        send_a.wait_send()
        send_b.wait_send()

    @pl.when(has_lower)
    def _():
        send_s.wait_send()
        send_f.wait_send()


def shards(n, activations, first_kernel, second_kernel, head_weight, labels):
    inverse_count = 1.0 / (labels.size * n)
    p1 = 8 * -(-144 // (8 * n))
    p2 = 8 * -(-432 // (8 * n))
    vmem = pl.BlockSpec(memory_space=pltpu.VMEM)
    dma = pltpu.SemaphoreType.DMA
    out, first, second, head = pl.pallas_call(
        functools.partial(kernel, n, p1, p2, inverse_count),
        out_shape=(
            jax.ShapeDtypeStruct((4, 256, 512), BF16),
            jax.ShapeDtypeStruct((432, 32), F32),
            jax.ShapeDtypeStruct((864, 64), F32),
            jax.ShapeDtypeStruct((1, 64), F32),
        ),
        in_specs=[vmem] * 5,
        out_specs=(vmem,) * 4,
        scratch_shapes=[
            pltpu.VMEM((5, 816, 256), BF16),
            pltpu.VMEM((3, 864, 128), BF16),
            pltpu.VMEM((640, 128), BF16),
            pltpu.VMEM((640, 128), BF16),
            pltpu.VMEM((3, 576, 256), BF16),
            pltpu.VMEM((2, 256, 256), F32),
            pltpu.VMEM((4, 256, 512), BF16),
            pltpu.VMEM((512, 640), BF16),
            pltpu.VMEM((512, 512), BF16),
            pltpu.VMEM((3, 32, 144), BF16),
            pltpu.VMEM((3, 64, 288), BF16),
            pltpu.VMEM((192, 128), BF16),
            pltpu.VMEM((384, 256), BF16),
            pltpu.VMEM((256, 256), BF16),
            pltpu.VMEM((256, 128), BF16),
            pltpu.VMEM((256, 256), BF16),
            pltpu.VMEM((256, 512), BF16),
            pltpu.VMEM((256, 256), BF16),
            pltpu.VMEM((256, 128), BF16),
            pltpu.VMEM((256, 256), BF16),
        ]
        + [pltpu.VMEM((n, p1, 128), F32)] * 3
        + [pltpu.VMEM((n, p2, 128), F32)] * 3
        + [dma((4,)), dma((4,))]
        + [dma((n,))] * 8,
        compiler_params=pltpu.CompilerParams(
            collective_id=0, has_side_effects=True, vmem_limit_bytes=40 * 1024 * 1024
        ),
    )(
        activations.reshape(4, 256, 512),
        first_kernel.reshape(432, 32),
        second_kernel.reshape(864, 64),
        head_weight.reshape(1, 64),
        labels,
    )
    return (
        out.reshape(activations.shape),
        first.reshape(first_kernel.shape),
        second.reshape(second_kernel.shape),
        head.reshape(head_weight.shape),
    )


def solution(mesh):
    return jax.shard_map(
        functools.partial(shards, mesh.shape["gx"]),
        mesh=mesh,
        in_specs=(
            P(("groups", "gx"), None, None, None),
            P(),
            P(),
            P(),
            P(("groups", "gx"), None, None),
        ),
        out_specs=(
            P(("groups", "gx"), None, None, None),
            P("groups", None, None, None, None),
            P("groups", None, None, None, None),
            P("groups"),
        ),
        check_vma=False,
    )
```

profile of v0, /device:TPU:0, one launch (start us, length us, event | category | flops | bytes accessed | tf_op | source)
XLA Modules:
  0.0 39.6 jit_solution(7827890476327981808)
XLA Ops:
  0.6 0.0 copy-start.3
  0.6 0.0 copy-start.4
  0.7 0.7 %copy-done.3 = s32[1,4,128]{2,1,0:T(4,128)S(1)} copy-done((s32[1,4,128]{2,1,0:T(4,128)S(1)}, s32[1,4,128]{2,1,0:T(4,128)}, u32[]{:S(2)}) %copy-start.3) | copy-done | bytes 2072
  1.3 0.0 copy-done.4
  1.3 0.0 copy-start
  1.3 1.2 %copy-done = bf16[4,16,16,512]{3,2,1,0:T(8,128)(2,1)S(1)} copy-done((bf16[4,16,16,512]{3,2,1,0:T(8,128)(2,1)S(1)}, bf16[4,16,16,512]{3,2,1,0:T(8,128)(2,1)}, u32[]{:S(2)}) %copy-start) | copy-done | bytes 1048600
  2.5 0.0 copy-start.1
  2.5 0.9 %copy-done.1 = bf16[3,3,3,32,64]{4,3,2,1,0:T(8,128)(2,1)S(1)} copy-done((bf16[3,3,3,32,64]{4,3,2,1,0:T(8,128)(2,1)S(1)}, bf16[3,3,3,32,64]{4,3,2,1,0:T(8,128)(2,1)}, u32[]{:S(2)}) %copy-start.1) | copy-done | bytes 110616
  3.5 0.0 copy-start.2
  3.5 0.9 %copy-done.2 = bf16[3,3,3,16,32]{4,3,2,1,0:T(8,128)(2,1)S(1)} copy-done((bf16[3,3,3,16,32]{4,3,2,1,0:T(8,128)(2,1)S(1)}, bf16[3,3,3,16,32]{4,3,2,1,0:T(8,128)(2,1)}, u32[]{:S(2)}) %copy-start.2) | copy-done | bytes 27672
  4.4 32.2 %shard_map.84 = (bf16[4,256,512]{2,1,0:T(8,128)(2,1)S(1)}, f32[432,32]{1,0:T(8,128)S(1)}, f32[864,64]{1,0:T(8,128)S(1)}, f32[1,64]{1,0:T(1,128)S(1)}) custom-call(bf16[4,256,512]{2,1,0:T(8,128)(2,1)S(1)} %bitcast.8, bf16[432,32]{1,0:T(8,128)(2,1)S(1)} %bitcast.13, bf16[864,64]{1,0:T(8,128)(2,1)S(1)} %bitcast.11, f32[1,64]{1,0:T(1,128)S(1)} %bitcast.14, ...), custom_call_target="tpu_custom_call" | custom-call | tf_op jit(solution)/shard_map/pallas_call | solution.py:394
  36.6 1.0 %copy.13 = bf16[4,16,16,512]{3,2,1,0:T(8,128)(2,1)} copy(bf16[4,16,16,512]{3,2,1,0:T(8,128)(2,1)S(1)} %bitcast.9) | data formatting | bytes 2097152
  37.6 0.7 %copy.14 = f32[3,3,3,16,32]{4,3,2,1,0:T(8,128)} copy(f32[3,3,3,16,32]{4,3,2,1,0:T(8,128)S(1)} %bitcast.12) | data formatting | bytes 110592
  38.3 0.8 %copy.15 = f32[3,3,3,32,64]{4,3,2,1,0:T(8,128)} copy(f32[3,3,3,32,64]{4,3,2,1,0:T(8,128)S(1)} %bitcast.10) | data formatting | bytes 442368
  39.0 0.5 %copy.16 = f32[64]{0:T(128)} copy(f32[64]{0:T(128)S(1)} %bitcast.15) | data formatting | bytes 512
Async XLA Ops:
  0.6 0.7 %copy-start.3 = (s32[1,4,128]{2,1,0:T(4,128)S(1)}, s32[1,4,128]{2,1,0:T(4,128)}, u32[]{:S(2)}) copy-start(s32[1,4,128]{2,1,0:T(4,128)} %labels.1) | copy-start | bytes 6148
  0.6 0.7 %copy-start.4 = (f32[64]{0:T(128)S(1)}, f32[64]{0:T(128)}, u32[]{:S(2)}) copy-start(f32[64]{0:T(128)} %param.8) | copy-start | bytes 772
  1.3 1.2 %copy-start = (bf16[4,16,16,512]{3,2,1,0:T(8,128)(2,1)S(1)}, bf16[4,16,16,512]{3,2,1,0:T(8,128)(2,1)}, u32[]{:S(2)}) copy-start(bf16[4,16,16,512]{3,2,1,0:T(8,128)(2,1)} %param.5) | copy-start | bytes 3145732
  2.5 0.9 %copy-start.1 = (bf16[3,3,3,32,64]{4,3,2,1,0:T(8,128)(2,1)S(1)}, bf16[3,3,3,32,64]{4,3,2,1,0:T(8,128)(2,1)}, u32[]{:S(2)}) copy-start(bf16[3,3,3,32,64]{4,3,2,1,0:T(8,128)(2,1)} %param.7) | copy-start | bytes 331780
  3.5 0.9 %copy-start.2 = (bf16[3,3,3,16,32]{4,3,2,1,0:T(8,128)(2,1)S(1)}, bf16[3,3,3,16,32]{4,3,2,1,0:T(8,128)(2,1)}, u32[]{:S(2)}) copy-start(bf16[3,3,3,16,32]{4,3,2,1,0:T(8,128)(2,1)} %param.6) | copy-start | bytes 82948
where the time goes:
time: 39.8 us; the launch traced here: 39.6 us
  Pallas kernels  32.2 us (81%)
  local copies, waits for them, and re-layouts  6.66 us (17%)
  between operations  0.66 us (2%)
    pallas_call x1, Pallas kernels, shards(): pl.pallas_call(functools.partial(kernel, n, p1, p2, inverse_count), out_s...  32.2 us
    unnamed x14, local copies, waits for them, and re-layouts  6.66 us

commit v1 on v0

--- a/solution.py
+++ b/solution.py
@@ -46,12 +46,13 @@
 
 
 def kernel(
-    n, p1, p2, inverse_count,
-    act, w1, w2, hw, labels,
-    out, fg_out, sg_out, head_out,
+    n, inverse_count,
+    act_hbm, w1_hbm, w2_hbm, hw_hbm, labels_hbm,
+    out_hbm, fg_out, sg_out, head_out,
     A, B, S2, SU, F2, slope1, IGp, spread, gather, w1t, w2t, bd1, bd2,
     abuf, sbuf, fbuf, halo_a, halo_b, halo_s, halo_f,
     G1, R1, T1, G2, R2, T2,
+    act, w1, w2, hw, labels, load, out,
     halo_send, halo_recv, rs1_s, rs1_r, ag1_s, ag1_r, rs2_s, rs2_r, ag2_s, ag2_r,
 ):
     me = lax.axis_index("gx")
@@ -70,6 +71,14 @@
 
     lax.fori_loop(1, n, greet, 0)
 
+    loads = [pltpu.make_async_copy(act_hbm.at[x], act.at[x], load.at[x]) for x in range(4)]
+    smalls = [
+        pltpu.make_async_copy(source, target, load.at[4 + k])
+        for k, (source, target) in enumerate(((w1_hbm, w1), (w2_hbm, w2), (hw_hbm, hw), (labels_hbm, labels)))
+    ]
+    for copy in smalls + [loads[x] for x in (1, 2, 3, 0)]:
+        copy.start()
+
     z_row = iota((512, 640), 0)
     lane = iota((512, 640), 1)
     spread[...] = one_hot(z_row == 4 * (lane & 127) + (lane >> 7) - 1)
@@ -86,7 +95,7 @@
 
     up = lax.rem(me + 1, n)
     down = lax.rem(me + n - 1, n)
-    send_a = halo(0, act.at[3], halo_a, up)
+    send_a = halo(0, act_hbm.at[3], halo_a, up)
     send_b = halo(1, abuf, halo_b, up)
     send_s = halo(2, sbuf, halo_s, down)
     send_f = halo(3, fbuf, halo_f, down)
@@ -94,6 +103,9 @@
     @pl.when(has_upper)
     def _():
         send_a.start()
+
+    for copy in smalls:
+        copy.wait()
 
     eye32 = one_hot(iota((32, 32), 0) == iota((32, 32), 1))
     eye64 = one_hot(iota((64, 64), 0) == iota((64, 64), 1))
@@ -162,6 +174,7 @@
         each(8, body)
 
     for x in (1, 2, 3):
+        loads[x].wait()
         fill_a(x + 1, act[x])
     first_section(1)
 
@@ -169,6 +182,7 @@
     def _():
         send_b.start()
 
+    loads[0].wait()
     fill_a(1, act[0])
 
     @pl.when(has_lower)
@@ -240,49 +254,115 @@
     def _():
         send_f.start()
 
+    def base(G):
+        return (n - G.shape[0]) // 2
+
+    def owns(G, device):
+        return jnp.logical_and(device >= base(G), device < base(G) + G.shape[0])
+
     def scatter(G, R, s_sem, r_sem):
         def step(d, carry):
             to = partner(d)
-            pltpu.make_async_remote_copy(
-                src_ref=G.at[to], dst_ref=R.at[me], send_sem=s_sem.at[d], recv_sem=r_sem.at[me],
-                device_id=(group, to), device_id_type=MESH,
-            ).start()
+
+            @pl.when(owns(G, to))
+            def _():
+                q = to - base(G)
+                pltpu.make_async_remote_copy(
+                    src_ref=G.at[q], dst_ref=R.at[me], send_sem=s_sem.at[q], recv_sem=r_sem.at[me],
+                    device_id=(group, to), device_id_type=MESH,
+                ).start()
+
             return carry
 
-        lax.fori_loop(1, n, step, 0)
-        R[me] = G[me]
-
-    def gather_total(G, R, T, s_sem, r_sem, t_s, t_r):
-        def arrive(d, carry):
-            other = partner(d)
-            pltpu.make_async_remote_copy(
-                src_ref=G.at[other], dst_ref=R.at[other], send_sem=s_sem.at[d], recv_sem=r_sem.at[other],
-                device_id=(group, other), device_id_type=MESH,
-            ).wait()
+        lax.fori_loop(1, n, step, 0, unroll=n <= 16)
+
+    def gather_total(G, R, T, s_sem, r_sem, t_s, t_r, split):
+        @pl.when(owns(G, me))
+        def _():
+            q = me - base(G)
+            R[me] = G[q]
+
+            def arrive(d, carry):
+                other = partner(d)
+                pltpu.make_async_remote_copy(
+                    src_ref=G.at[q], dst_ref=R.at[other], send_sem=s_sem.at[q], recv_sem=r_sem.at[other],
+                    device_id=(group, other), device_id_type=MESH,
+                ).wait_recv()
+                return carry
+
+            lax.fori_loop(1, n, arrive, 0)
+            total = jnp.sum(R[...].astype(F32), axis=0)
+            if split:
+                total = join(total)
+            T[q] = total.astype(BF16) if not split else halves(total)
+
+            def step(d, carry):
+                to = partner(d)
+                pltpu.make_async_remote_copy(
+                    src_ref=T.at[q], dst_ref=T.at[q], send_sem=t_s.at[to], recv_sem=t_r.at[q],
+                    device_id=(group, to), device_id_type=MESH,
+                ).start()
+                return carry
+
+            lax.fori_loop(1, n, step, 0, unroll=n <= 16)
+
+    def collect(T, t_s, t_r):
+        def arrive(q, carry):
+            source = q + base(T)
+
+            @pl.when(source != me)
+            def _():
+                pltpu.make_async_remote_copy(
+                    src_ref=T.at[q], dst_ref=T.at[q], send_sem=t_s.at[source], recv_sem=t_r.at[q],
+                    device_id=(group, source), device_id_type=MESH,
+                ).wait_recv()
+
             return carry
 
-        lax.fori_loop(1, n, arrive, 0)
-        T[me] = jnp.sum(R[...], axis=0)
-
-        def step(d, carry):
-            pltpu.make_async_remote_copy(
-                src_ref=T.at[me], dst_ref=T.at[me], send_sem=t_s.at[d], recv_sem=t_r.at[me],
-                device_id=(group, partner(d)), device_id_type=MESH,
-            ).start()
+        lax.fori_loop(0, T.shape[0], arrive, 0)
+
+    def drain(G, R, T, s_sem, r_sem, t_s, t_r):
+        def sent(q, carry):
+            to = q + base(G)
+
+            @pl.when(to != me)
+            def _():
+                pltpu.make_async_remote_copy(
+                    src_ref=G.at[q], dst_ref=R.at[me], send_sem=s_sem.at[q], recv_sem=r_sem.at[me],
+                    device_id=(group, to), device_id_type=MESH,
+                ).wait_send()
+
             return carry
 
-        lax.fori_loop(1, n, step, 0)
-
-    def collect(T, t_s, t_r):
-        def arrive(d, carry):
-            other = partner(d)
-            pltpu.make_async_remote_copy(
-                src_ref=T.at[me], dst_ref=T.at[other], send_sem=t_s.at[d], recv_sem=t_r.at[other],
-                device_id=(group, other), device_id_type=MESH,
-            ).wait()
-            return carry
-
-        lax.fori_loop(1, n, arrive, 0)
+        lax.fori_loop(0, G.shape[0], sent, 0)
+
+        @pl.when(owns(G, me))
+        def _():
+            q = me - base(G)
+
+            def step(d, carry):
+                to = partner(d)
+                pltpu.make_async_remote_copy(
+                    src_ref=T.at[q], dst_ref=T.at[q], send_sem=t_s.at[to], recv_sem=t_r.at[q],
+                    device_id=(group, to), device_id_type=MESH,
+                ).wait_send()
+                return carry
+
+            lax.fori_loop(1, n, step, 0)
+
+    def join(value):
+        return value + jnp.where(iota(value.shape, 1) == 96, pltpu.roll(value, 127, axis=1), 0.0)
+
+    def halves(value):
+        rounded = value.astype(BF16).astype(F32)
+        rest = pltpu.roll(value - rounded, 1, axis=1)
+        return jnp.where(iota(value.shape, 1) == 97, rest, rounded).astype(BF16)
+
+    def pack(value, G):
+        flat = G.shape[0] * G.shape[1]
+        if flat > value.shape[0]:
+            value = jnp.concatenate((value, jnp.zeros((flat - value.shape[0], 128), BF16)), axis=0)
+        G[...] = value.reshape(G.shape)
 
     sums = []
     for a in range(3):
@@ -297,8 +377,7 @@
         ),
         axis=1,
     )
-    packed = jnp.concatenate((packed, jnp.zeros((n * p2 - 432, 128), F32)), axis=0)
-    G2[...] = packed.reshape(n, p2, 128)
+    pack(packed.astype(BF16), G2)
     scatter(G2, R2, rs2_s, rs2_r)
 
     @pl.when(has_upper)
@@ -324,9 +403,14 @@
     head_column = jnp.concatenate((head, jnp.zeros((80, 1), F32)), axis=0)
     packed = jnp.concatenate(
         [first_grad(a) for a in range(3)] + [jnp.broadcast_to(head_column, (144, 32))], axis=1)
-    packed = jnp.concatenate((packed, jnp.zeros((n * p1 - 144, 128), F32)), axis=0)
-    G1[...] = packed.reshape(n, p1, 128)
+    pack(halves(packed), G1)
     scatter(G1, R1, rs1_s, rs1_r)
+
+    stores = [pltpu.make_async_copy(out.at[x], out_hbm.at[x], load.at[x]) for x in range(4)]
+
+    def store(x):
+        out[x] = mm(IGp[x], gather[...]).astype(BF16)
+        stores[x].start()
 
     def put(x, j, value):
         value = value.astype(BF16)
@@ -343,10 +427,10 @@
         put(2, j, high[0:64, :])
 
     each(8, own_planes)
-    gather_total(G2, R2, T2, rs2_s, rs2_r, ag2_s, ag2_r)
+    gather_total(G2, R2, T2, rs2_s, rs2_r, ag2_s, ag2_r, False)
     for x in range(3):
-        out[x] = mm(IGp[x], gather[...]).astype(BF16)
-    gather_total(G1, R1, T1, rs1_s, rs1_r, ag1_s, ag1_r)
+        store(x)
+    gather_total(G1, R1, T1, rs1_s, rs1_r, ag1_s, ag1_r, True)
 
     @pl.when(has_upper)
     def _():
@@ -362,17 +446,17 @@
         put(3, j, mm(bd1[64:128, :], F2[1, at, :]) + mm(bd1[128:192, :], F2[2, at, :]))
 
     each(8, last_plane)
-    out[3] = mm(IGp[3], gather[...]).astype(BF16)
+    store(3)
 
     collect(T2, ag2_s, ag2_r)
-    second = T2[...].reshape(n * p2, 128)
+    second = T2[...].astype(F32).reshape(-1, 128)
     sg_out[0:432, :] = second[0:432, 0:64]
     sg_out[432:864, :] = second[0:432, 64:128]
     collect(T1, ag1_s, ag1_r)
-    first = T1[...].reshape(n * p1, 128)
+    first = T1[...].astype(F32).reshape(-1, 128)
     for a in range(3):
         fg_out[a * 144:(a + 1) * 144, :] = first[0:144, a * 32:(a + 1) * 32]
-    head_out[...] = jnp.sum(jnp.where(diagonal, first[0:64, 96:97], 0.0), axis=0, keepdims=True)
+    head_out[...] = jnp.sum(jnp.where(diagonal, join(first)[0:64, 96:97], 0.0), axis=0, keepdims=True)
 
     @pl.when(has_upper)
     def _():
@@ -384,23 +468,35 @@
         send_s.wait_send()
         send_f.wait_send()
 
+    for copy in stores:
+        copy.wait()
+    drain(G2, R2, T2, rs2_s, rs2_r, ag2_s, ag2_r)
+    drain(G1, R1, T1, rs1_s, rs1_r, ag1_s, ag1_r)
+
+
+def cut(units, n):
+    size = -(-units // n)
+    return -(-units // size), 16 * size
+
 
 def shards(n, activations, first_kernel, second_kernel, head_weight, labels):
     inverse_count = 1.0 / (labels.size * n)
-    p1 = 8 * -(-144 // (8 * n))
-    p2 = 8 * -(-432 // (8 * n))
+    q1, p1 = cut(9, n)
+    q2, p2 = cut(27, n)
     vmem = pl.BlockSpec(memory_space=pltpu.VMEM)
     dma = pltpu.SemaphoreType.DMA
+    hbm = pl.BlockSpec(memory_space=pltpu.HBM)
+    results = (
+        jax.ShapeDtypeStruct((4, 256, 512), BF16),
+        jax.ShapeDtypeStruct((432, 32), F32),
+        jax.ShapeDtypeStruct((864, 64), F32),
+        jax.ShapeDtypeStruct((1, 64), F32),
+    )
     out, first, second, head = pl.pallas_call(
-        functools.partial(kernel, n, p1, p2, inverse_count),
-        out_shape=(
-            jax.ShapeDtypeStruct((4, 256, 512), BF16),
-            jax.ShapeDtypeStruct((432, 32), F32),
-            jax.ShapeDtypeStruct((864, 64), F32),
-            jax.ShapeDtypeStruct((1, 64), F32),
-        ),
-        in_specs=[vmem] * 5,
-        out_specs=(vmem,) * 4,
+        functools.partial(kernel, n, inverse_count),
+        out_shape=results,
+        in_specs=[hbm] * 5,
+        out_specs=(hbm, vmem, vmem, vmem),
         scratch_shapes=[
             pltpu.VMEM((5, 816, 256), BF16),
             pltpu.VMEM((3, 864, 128), BF16),
@@ -423,12 +519,22 @@
             pltpu.VMEM((256, 128), BF16),
             pltpu.VMEM((256, 256), BF16),
         ]
-        + [pltpu.VMEM((n, p1, 128), F32)] * 3
-        + [pltpu.VMEM((n, p2, 128), F32)] * 3
+        + [pltpu.VMEM((pieces, p1, 128), BF16) for pieces in (q1, n, q1)]
+        + [pltpu.VMEM((pieces, p2, 128), BF16) for pieces in (q2, n, q2)]
+        + [
+            pltpu.VMEM((4, 256, 512), BF16),
+            pltpu.VMEM((432, 32), BF16),
+            pltpu.VMEM((864, 64), BF16),
+            pltpu.VMEM((1, 64), F32),
+            pltpu.VMEM(labels.shape, labels.dtype),
+            dma((8,)),
+            pltpu.VMEM((4, 256, 512), BF16),
+        ]
         + [dma((4,)), dma((4,))]
-        + [dma((n,))] * 8,
+        + [dma((q1,)), dma((n,)), dma((n,)), dma((q1,))]
+        + [dma((q2,)), dma((n,)), dma((n,)), dma((q2,))],
         compiler_params=pltpu.CompilerParams(
-            collective_id=0, has_side_effects=True, vmem_limit_bytes=40 * 1024 * 1024
+            collective_id=0, has_side_effects=True, vmem_limit_bytes=63 * 1024 * 1024
         ),
     )(
         activations.reshape(4, 256, 512),

time: 39.8 us -> 32.9 us (0.83)
  Pallas kernels: 32.2 us -> 27.4 us
  local copies, waits for them, and re-layouts: 6.66 us -> 4.68 us
    pallas_call x1, Pallas kernels: 32.2 us -> 27.4 us  [shards(): pl.pallas_call(functools.partial(kernel, n, inverse_count), out_shape=res...]
    unnamed x14 -> x10, local copies, waits for them, and re-layouts: 6.66 us -> 4.68 us
where the time goes in v1:
time: 32.9 us; the launch traced here: 32.7 us
  Pallas kernels  27.4 us (83%)
  local copies, waits for them, and re-layouts  4.68 us (14%)
  between operations  0.65 us (2%)
    pallas_call x1, Pallas kernels, shards(): pl.pallas_call(functools.partial(kernel, n, inverse_count), out_shape=res...  27.4 us
    unnamed x10, local copies, waits for them, and re-layouts  4.68 us

profile of v1, /device:TPU:0, one launch (start us, length us, event | category | flops | bytes accessed | tf_op | source)
XLA Modules:
  0.0 32.7 jit_solution(7636298721497606834)
XLA Ops:
  0.6 27.4 %shard_map.84 = (bf16[4,256,512]{2,1,0:T(8,128)(2,1)}, f32[432,32]{1,0:T(8,128)}, f32[864,64]{1,0:T(8,128)}, f32[1,64]{1,0:T(1,128)}) custom-call(bf16[4,256,512]{2,1,0:T(8,128)(2,1)} %bitcast.8, bf16[432,32]{1,0:T(8,128)(2,1)} %bitcast.13, bf16[864,64]{1,0:T(8,128)(2,1)} %bitcast.11, f32[1,64]{1,0:T(1,128)} %bitcast.14, s32[1,4,128]{2,1,0:T(4,128)} %labels_hbm.1), custom_call_target="tpu_custom_call" | custom-call | tf_op jit(solution)/shard_map/pallas_call | solution.py:495
  28.1 0.0 copy-start.1
  28.1 2.3 %copy.13 = bf16[4,16,16,512]{3,2,1,0:T(8,128)(2,1)} copy(bf16[4,16,16,512]{3,2,1,0:T(8,128)(2,1)} %bitcast.9) | data formatting | bytes 2097152
  30.4 0.0 copy-done.1
  30.4 0.0 copy-start
  30.4 0.7 %copy.14 = f32[3,3,3,16,32]{4,3,2,1,0:T(8,128)} copy(f32[3,3,3,16,32]{4,3,2,1,0:T(8,128)S(1)} %bitcast.12) | data formatting | bytes 110592
  31.1 0.4 %copy-done = f32[864,64]{1,0:T(8,128)S(1)} copy-done((f32[864,64]{1,0:T(8,128)S(1)}, f32[864,64]{1,0:T(8,128)}, u32[]{:S(2)}) %copy-start) | copy-done | bytes 221208
  31.5 0.0 copy-start.2
  31.5 0.8 %copy.15 = f32[3,3,3,32,64]{4,3,2,1,0:T(8,128)} copy(f32[3,3,3,32,64]{4,3,2,1,0:T(8,128)S(1)} %bitcast.10) | data formatting | bytes 442368
  32.2 0.0 copy-done.2
  32.2 0.5 %copy.16 = f32[64]{0:T(128)} copy(f32[64]{0:T(128)S(1)} %bitcast.15) | data formatting | bytes 512
Async XLA Ops:
  28.1 2.3 %copy-start.1 = (f32[432,32]{1,0:T(8,128)S(1)}, f32[432,32]{1,0:T(8,128)}, u32[]{:S(2)}) copy-start(f32[432,32]{1,0:T(8,128)} %get-tuple-element.9) | copy-start | bytes 165892
  30.4 1.1 %copy-start = (f32[864,64]{1,0:T(8,128)S(1)}, f32[864,64]{1,0:T(8,128)}, u32[]{:S(2)}) copy-start(f32[864,64]{1,0:T(8,128)} %get-tuple-element.10) | copy-start | bytes 663556
  31.5 0.8 %copy-start.2 = (f32[1,64]{1,0:T(1,128)S(1)}, f32[1,64]{1,0:T(1,128)}, u32[]{:S(2)}) copy-start(f32[1,64]{1,0:T(1,128)} %get-tuple-element.11) | copy-start | bytes 772
